TPU v7x, 128 devices: a whole 4x4x4 slice. The times are simulated.
128 devices in a mesh: band: 2 (over x_lo), domain: 64 (over z, y, x_hi, core).
Axes of the slice: x: 4 (x_hi: 2, x_lo: 2; x = x_hi * 2 + x_lo), y: 4, z: 4, core: 2. Of those that a mesh axis runs over, the one named last changes fastest.
Arguments:
- orbitals: float32 [32, 512, 32, 128], P('band', 'domain'), may hold values from -6 to 6
- potential: float32 [512, 32, 128], P('domain'), may hold values from -2 to 1
- earlier: float32 [128, 512, 32, 128], P('band', 'domain'), may hold values from -6 to 6
- incoming: float32 [64, 512, 32, 128], P('band', 'domain'), may hold values from -64 to 64
Outputs:
- applied: float32 [32, 512, 32, 128], P('band', 'domain')
- correlations: float32 [128, 64], P('band')
- orthonormal: float32 [64, 512, 32, 128], P('band', 'domain')
All inputs are finite; a program needn't handle non-finite values.
Results may differ from a plain program's by a relative error of at most 0.00015.
Values sent between devices are 32-bit elements; how exact they have to be, the bound alone decides.
A program may use at most 128 MiB of HBM per device.

v0:
```python
import jax
import jax.numpy as jnp
from jax import lax
from jax.sharding import PartitionSpec as P

coeffs = (
    -5369.0 / 1800.0,
    12.0 / 7.0,
    -15.0 / 56.0,
    10.0 / 189.0,
    -1.0 / 112.0,
    2.0 / 1925.0,
    -1.0 / 16632.0,
)


def padded_2(cells, sides, width):
    for axis, dim in sides:
        count = lax.axis_size(axis)
        head = lax.slice_in_dim(cells, 0, width, axis=dim)
        tail = lax.slice_in_dim(cells, cells.shape[dim] - width, cells.shape[dim], axis=dim)
        cells = jnp.concatenate(
            [
                lax.ppermute(tail, axis, [(i, (i + 1) % count) for i in range(count)]),
                cells,
                lax.ppermute(head, axis, [((i + 1) % count, i) for i in range(count)]),
            ],
            axis=dim,
        )
    return cells


def laplace(field):
    depth = 6
    planes = field.shape[1]
    width_y = field.shape[2]
    width_z = field.shape[3]
    extended = padded_2(field, (("domain", 1),), depth)
    padded = jnp.pad(field, ((0, 0), (0, 0), (depth, depth), (depth, depth)))
    total = 3.0 * coeffs[0] * field
    for step in range(1, depth + 1):
        total = total + coeffs[step] * (
            extended[:, depth + step : depth + step + planes]
            + extended[:, depth - step : depth - step + planes]
        )
        total = total + coeffs[step] * (
            padded[:, :, depth + step : depth + step + width_y, depth : depth + width_z]
            + padded[:, :, depth - step : depth - step + width_y, depth : depth + width_z]
        )
        total = total + coeffs[step] * (
            padded[:, :, depth : depth + width_y, depth + step : depth + step + width_z]
            + padded[:, :, depth : depth + width_y, depth - step : depth - step + width_z]
        )
    return total


def on_device(orbitals, potential, earlier, incoming):
    high = lax.Precision.HIGHEST
    applied = -0.5 * laplace(orbitals) + potential[None] * orbitals
    mine_rows = incoming.shape[0]
    planes = incoming.shape[1]
    ncells = lax.axis_size("domain") * planes * incoming.shape[2] * incoming.shape[3]
    prev_flat = earlier.reshape(earlier.shape[0], -1)
    mine_flat = incoming.reshape(mine_rows, -1)
    gathered = lax.all_gather(mine_flat, "band", axis=0, tiled=True)
    partial_correlations = (
        jnp.dot(prev_flat, gathered.T, precision=high, preferred_element_type=jnp.float32) / ncells
    )
    correlations = lax.psum(partial_correlations, "domain")
    removed = lax.psum_scatter(
        jnp.dot(correlations.T, prev_flat, precision=high, preferred_element_type=jnp.float32),
        "band",
        scatter_dimension=0,
        tiled=True,
    )
    cleaned = lax.all_gather(mine_flat - removed, "band", axis=0, tiled=True)
    partial_gram = (
        jnp.dot(cleaned, cleaned.T, precision=high, preferred_element_type=jnp.float32) / ncells
    )
    gram = lax.psum(partial_gram, "domain")
    factor = jnp.linalg.cholesky(gram)
    total_rows = gram.shape[0]
    inverse = jax.scipy.linalg.solve_triangular(
        factor, jnp.eye(total_rows, dtype=jnp.float32), lower=True
    )
    first = lax.axis_index("band") * mine_rows
    inverse_rows = lax.dynamic_slice_in_dim(inverse, first, mine_rows, 0)
    orthonormal = jnp.dot(inverse_rows, cleaned, precision=high, preferred_element_type=jnp.float32)
    return (applied, correlations, orthonormal.reshape(incoming.shape))


def solution(mesh):
    in_specs = (
        P("band", "domain", None, None),
        P("domain", None, None),
        P("band", "domain", None, None),
        P("band", "domain", None, None),
    )
    out_specs = (P("band", "domain", None, None), P("band", None), P("band", "domain", None, None))
    return jax.shard_map(
        on_device, mesh=mesh, in_specs=in_specs, out_specs=out_specs, check_vma=False
    )
```

profile of v0, /device:TPU:1, one launch (start us, length us, event | category | flops | bytes accessed | tf_op | source)
XLA Modules:
  0.0 1082.7 jit_solution(5611014000268338614)
XLA Ops:
  7.2 0.0 all-gather.3.cloned.1.call-start
  7.2 6.6 copy.29
  13.9 0.0 reduce-scatter.2.cloned.1.call-start
  13.9 109.8 %all-gather.3.cloned.1.call-done = f32[64,32768]{1,0:T(8,128)} async-done(((f32[32,32768]{1,0:T(8,128)}), f32[64,32768]{1,0:T(8,128)}) %all-gather.3.cloned.1.call-update) | async-done | bytes 8388624 | tf_op jit(solution)/shard_map/all_gather | solution.py:65
  123.8 16.9 %fusion.54 = f32[64,64]{0,1:T(8,128)S(1)} fusion(f32[64,32768]{1,0:T(8,128)} %all-gather.3.cloned.1.call-done, f32[8,8,256,128]{3,2,1,0:T(8,128)} %bitcast.34), kind=kOutput, calls=%fused_computation.87 | convolution fusion | flops 1610616832 | bytes 16793600 | tf_op jit(solution)/shard_map/dot_general | solution.py:67
  140.7 322.6 %psum.14 = f32[64,64]{0,1:T(8,128)S(1)} all-reduce(f32[64,64]{0,1:T(8,128)S(1)} %fusion.54), channel_id=1, replica_groups=mesh['band'=2,'domain'=64] {'domain'}, use_global_device_ids=true, to_apply=%region_0.1 | all-reduce | flops 4096 | bytes 32768 | tf_op jit(solution)/shard_map/psum | solution.py:69
  463.2 17.4 %fusion = f32[64,32768]{1,0:T(8,128)} fusion(f32[64,64]{0,1:T(8,128)S(1)} %psum.14, f32[8,8,256,128]{3,2,1,0:T(8,128)} %bitcast.35), kind=kOutput, calls=%fused_computation.24 | convolution fusion | flops 1610612736 | bytes 16793600 | tf_op jit(solution)/shard_map/dot_general | solution.py:71
  480.6 0.0 all-gather.5.cloned.1.call-start
  480.7 102.7 %reduce-scatter.2.cloned.1.call-done = f32[32,32768]{1,0:T(8,128)} async-done(((f32[64,32768]{1,0:T(8,128)}), f32[32,32768]{1,0:T(8,128)}) %reduce-scatter.2.cloned.1.call-update) | async-done | bytes 4194320 | tf_op jit(solution)/shard_map/reduce_scatter | solution.py:70
  583.4 8.0 fusion.63
  591.4 0.0 all-gather.5.cloned.1.call-update
  591.4 1.6 copy-done
  593.0 2.2 fusion.64
  595.1 3.0 collective-permute-start.1
  598.1 49.1 %collective-permute-done.1 = f32[16,6,32,128]{3,2,1,0:T(8,128)} collective-permute-done((f32[16,6,32,128]{3,2,1,0:T(8,128)}, f32[16,6,32,128]{3,2,1,0:T(8,128)}, u32[]{:S(2)}, u32[]{:S(2)}) %collective-permute-start.1) | collective-permute-done | bytes 1572896 | tf_op jit(solution)/shard_map/ppermute | solution.py:24
  647.2 1.6 constant_dynamic-update-slice_fusion.3
  648.7 0.5 constant_dynamic-update-slice_fusion.1
  649.3 11.3 %collective-permute-done = f32[16,6,32,128]{3,2,1,0:T(8,128)} collective-permute-done((f32[16,6,32,128]{3,2,1,0:T(8,128)}, f32[16,6,32,128]{3,2,1,0:T(8,128)}, u32[]{:S(2)}, u32[]{:S(2)}) %collective-permute-start) | collective-permute-done | bytes 1572896 | tf_op jit(solution)/shard_map/ppermute | solution.py:26
  660.6 1.6 constant_dynamic-update-slice_fusion
  662.2 7.7 multiply_add_fusion
  669.9 0.7 copy.10
  670.6 52.7 %all-gather.5.cloned.1.call-done = f32[64,32768]{1,0:T(8,128)} async-done(((f32[32,32768]{1,0:T(8,128)}), f32[64,32768]{1,0:T(8,128)}) %all-gather.5.cloned.1.call-update) | async-done | bytes 8388624 | tf_op jit(solution)/shard_map/all_gather | solution.py:76
  723.3 10.5 convolution_multiply_fusion
  733.7 320.9 %psum.15 = f32[64,64]{0,1:T(8,128)S(1)} all-reduce(f32[64,64]{0,1:T(8,128)S(1)} %convolution_multiply_fusion), channel_id=1, replica_groups=mesh['band'=2,'domain'=64] {'domain'}, use_global_device_ids=true, to_apply=%region_2.3 | all-reduce | flops 4096 | bytes 32768 | tf_op jit(solution)/shard_map/psum | solution.py:80
  1054.6 0.1 copy.9
  1054.7 5.8 cholesky.17
  1060.6 0.6 compare_reduce_fusion
  1061.2 0.7 fusion.57
  1061.9 4.9 custom-call.7
  1066.8 0.2 fusion.58
  1067.0 6.4 convolution_bitcast_fusion
  1073.5 2.8 copy.15
  (8 shorter events, 0.1 us)
Async XLA Ops:
  7.2 116.6 %all-gather.3.cloned.1.call-start = ((), (), s32[]{:S(2)}) async-start(), calls=%async_computation.1 | async-start | bytes 12582912 | tf_op jit(solution)/shard_map/all_gather | solution.py:65
  13.9 569.5 %reduce-scatter.2.cloned.1.call-start = ((), (), s32[]{:S(2)}) async-start(), calls=%async_computation.2 | async-start | bytes 12582912 | tf_op jit(solution)/shard_map/reduce_scatter | solution.py:70
  480.6 242.7 %all-gather.5.cloned.1.call-start = ((), (), s32[]{:S(2)}) async-start(), calls=%async_computation.3 | async-start | bytes 12582912 | tf_op jit(solution)/shard_map/all_gather | solution.py:76
  591.4 1.6 copy-start
  595.1 52.0 %collective-permute-start.1 = (f32[16,6,32,128]{3,2,1,0:T(8,128)}, f32[16,6,32,128]{3,2,1,0:T(8,128)}, u32[]{:S(2)}, u32[]{:S(2)}) collective-permute-start(f32[16,6,32,128]{3,2,1,0:T(8,128)} %get-tuple-element.7), channel_id=1, source_target_pairs={{0,1},{1,2},{2,3},{3,4},{4,5},{5,6},{6,7},{7,8},{8,9},{9,10},{10,1... | collective-permute-start | bytes 4718600 | tf_op jit(solution)/shard_map/ppermute | solution.py:24
  598.1 62.5 %collective-permute-start = (f32[16,6,32,128]{3,2,1,0:T(8,128)}, f32[16,6,32,128]{3,2,1,0:T(8,128)}, u32[]{:S(2)}, u32[]{:S(2)}) collective-permute-start(f32[16,6,32,128]{3,2,1,0:T(8,128)} %get-tuple-element.6), channel_id=1, source_target_pairs={{1,0},{2,1},{3,2},{4,3},{5,4},{6,5},{7,6},{8,7},{9,8},{10,9},{11,1... | collective-permute-start | bytes 4718600 | tf_op jit(solution)/shard_map/ppermute | solution.py:26
  649.3 12.9 %copy-start.1 = (f32[8,32,128]{2,1,0:T(8,128)S(1)}, f32[8,32,128]{2,1,0:T(8,128)}, u32[]{:S(2)}) copy-start(f32[8,32,128]{2,1,0:T(8,128)} %param.5) | copy-start | bytes 393220
Sparse Core Ops, SparseCore 0:
  14.0 109.7 all-gather.2
  480.8 102.5 reduce-scatter.1
  591.5 131.7 all-gather.4
where the time goes:
time: 1090 us; the launch traced here: 1080 us
  blocking collectives  643 us (59%)
  waiting for transfers between devices  326 us (30%)
  matrix products  51.4 us (5%)
  other arithmetic  27.8 us (3%)
  local copies, waits for them, and re-layouts  17.5 us (2%)
  between operations  13.8 us (1%)
    psum x1, blocking collectives, on_device(): correlations = lax.psum(partial_correlations, 'domain')  323 us
    psum x1, blocking collectives, on_device(): gram = lax.psum(partial_gram, 'domain')  321 us
    all_gather x1, waiting for transfers between devices, on_device(): gathered = lax.all_gather(mine_flat, 'band', axis=0, tiled=True)  110 us
    reduce_scatter x1, waiting for transfers between devices, on_device(): lax.psum_scatter(jnp.dot(correlations.T, prev_flat, precision=high, prefe...  103 us
    all_gather x1, waiting for transfers between devices, on_device(): cleaned = lax.all_gather(mine_flat - removed, 'band', axis=0, tiled=True)  52.7 us
    ppermute x1, waiting for transfers between devices, padded_2(): lax.ppermute(tail, axis, [(i, (i + 1) % count) for i in range(count)])  49.1 us
  transfers between devices with their start and end apart: 5, of which 5 were waited for; matrix products, arithmetic and copies ran while one was open for 1% of the time, Pallas kernels for 0%

commit v1 on v0

v1 whole, which is shorter than its diff:
```python
import jax
import jax.numpy as jnp
from jax import lax
from jax.experimental import pallas as pl
from jax.experimental.pallas import tpu as pltpu
from jax.sharding import PartitionSpec as P

coeffs = (
    -5369.0 / 1800.0,
    12.0 / 7.0,
    -15.0 / 56.0,
    10.0 / 189.0,
    -1.0 / 112.0,
    2.0 / 1925.0,
    -1.0 / 16632.0,
)

MESH = pl.DeviceIdType.MESH
HIGH = lax.Precision.HIGHEST
F32 = jnp.float32
BF16 = jnp.bfloat16

ORB = 16
PREV = 64
NEW = 32
PLANES = 8
KEPT = 4
CY = 32
CZ = 128
DEPTH = 6
ROWS = 2 * PREV + 2 * NEW
CELLS = KEPT * CY * CZ
TOTAL = 512 * CY * CZ

CHUNKS = 16
CHUNK_Y = KEPT * CY // CHUNKS
AHEAD = 2
NEAR = -(-ORB // (CHUNKS - 1))
PIECES = 2
TILES = 16
TILE_Y = KEPT * CY // TILES


def nt(a, b, precision=None):
    return lax.dot_general(
        a, b, (((1,), (1,)), ((), ())), precision=precision, preferred_element_type=F32
    )


def nn(a, b, precision=None):
    return lax.dot_general(
        a, b, (((1,), (0,)), ((), ())), precision=precision, preferred_element_type=F32
    )


def split(a):
    hi = a.astype(BF16)
    return hi, (a - hi.astype(F32)).astype(BF16)


def band_matrix(size, block, diagonal):
    i = lax.broadcasted_iota(jnp.int32, (size, size), 0)
    j = lax.broadcasted_iota(jnp.int32, (size, size), 1)
    gap = jnp.abs(i - j)
    out = jnp.where(gap == 0, diagonal, 0.0).astype(F32)
    for step in range(1, DEPTH + 1):
        out = jnp.where(gap == step, -0.5 * coeffs[step], out)
    if block != size:
        out = jnp.where(i // block == j // block, out, 0.0)
    return out


def kernel(
    orb, pot, earl, inc,
    applied, corr, ortho,
    to_give, rows, high, low, ext, potv, relay, grams, red,
    got_z, sum_z, got_y, part, twin_part, pair, got_x, whole_y, whole, work, factor, outs, band_z, band_y,
    s1, r1, l1, l0,
    s_in, r_in, s_out, r_relay, s_fwd, r_out,
    sz, rz, sy, ry, s_twin, r_twin, sx, rx, sgy, rgy, sgz, rgz,
    s2, r2, go, all_in,
):
    band = lax.axis_index("band")
    domain = lax.axis_index("domain")
    core = domain % 2
    x = ((domain // 2) % 2) * 2 + band
    y = (domain // 4) % 4
    z = domain // 16
    other = 1 - band

    def device(xx, yy, zz, cc):
        return (xx % 2, ((zz * 4 + yy) * 2 + xx // 2) * 2 + cc)

    z_peers = [device(x, y, (z + d) % 4, core) for d in range(1, 4)]
    y_peers = [device(x, (y + d) % 4, z, core) for d in range(1, 4)]
    partner = (other, domain)
    twin = (band, domain + 1 - 2 * core)
    toward = 2 * core - 1
    early = (band + core + 1) % 2
    next_domain = (domain + toward + 64) % 64
    via_y = early * ((next_domain // 4) % 4) + (1 - early) * y
    via_z = early * (next_domain // 16) + (1 - early) * z
    relayer = device((x + toward + 4) % 4, via_y, via_z, 1 - core)
    from_domain = ((z * 4 + y) * 2 + ((x + toward + 4) % 4) // 2) * 2 + 1 - core
    straight = ((z * 4 + y) * 2 + ((x - toward + 4) % 4) // 2) * 2 + core
    to_domain = (early * straight + (1 - early) * (from_domain - toward) + 64) % 64
    forward = (other, to_domain)
    way = 2 * band - 1
    chip = (z * 4 + y) * 2
    to = (chip + x // 2) * 2 + band + way + 64
    to = to % 64
    chip_passer = device(
        (((to // 2) % 2) * 2 + band - way + 4) % 4, (to // 4) % 4, to // 16, 1
    )
    giver_domain = ((chip + ((x - way + 4) % 4) // 2) * 2 + band + way + 64) % 64
    chip_giver = (other, giver_domain - giver_domain % 2 + 1)
    early = early == 1

    def piece(k):
        plane = k // (CY // CHUNK_Y)
        return plane, pl.ds(pl.multiple_of((k % (CY // CHUNK_Y)) * CHUNK_Y, CHUNK_Y), CHUNK_Y)

    def stage(k):
        plane, at = piece(k)
        return (
            pltpu.make_async_copy(
                earl.at[:, KEPT * other + plane, at], to_give.at[0:PREV, plane, at], l1.at[k, 0]
            ),
            pltpu.make_async_copy(
                inc.at[:, KEPT * other + plane, at], to_give.at[PREV:, plane, at], l1.at[k, 1]
            ),
        )

    def stage_all(k, _):
        for copy in stage(k):
            copy.start()
        return 0

    barrier = pltpu.get_barrier_semaphore()
    first, second = core == 0, core == 1

    def greet(peer):
        pl.semaphore_signal(barrier, inc=1, device_id=peer, device_id_type=MESH)

    def tell(semaphore):
        pl.semaphore_signal(semaphore, inc=1, device_id=twin, device_id_type=MESH)

    @pl.when(second)
    def _():
        greet(twin)
        greet((other, domain - 1))

    @pl.when(first)
    def _():
        greet(partner)

    lax.fori_loop(0, CHUNKS, stage_all, 0)

    @pl.when(first)
    def _():
        pl.semaphore_wait(barrier, 3)
        tell(go)

    @pl.when(second)
    def _():
        pl.semaphore_wait(go, 1)

    def remote(src, dst, send, recv, peer):
        return pltpu.make_async_remote_copy(
            src_ref=src, dst_ref=dst, send_sem=send, recv_sem=recv,
            device_id=peer, device_id_type=MESH,
        )

    def give(k):
        plane, at = piece(k)
        return (
            remote(
                to_give.at[0:PREV, plane, at],
                rows.at[pl.ds(PREV * band, PREV), plane, at],
                s1.at[k, 0], r1.at[k, 0], partner,
            ),
            remote(
                to_give.at[PREV:, plane, at],
                rows.at[pl.ds(2 * PREV + NEW * band, NEW), plane, at],
                s1.at[k, 1], r1.at[k, 1], partner,
            ),
        )

    for k in range(AHEAD):
        for copy in stage(k):
            copy.wait()
        for copy in give(k):
            copy.start()

    @pl.when(second)
    def _():
        for d in range(1, 4):
            greet(device(x, y, (z + d) % 4, 1))
            greet(device(x, (y + d) % 4, z, 1))
            greet(device((x + d) % 4, y, z, 1))
        greet(chip_passer)
        greet(chip_giver)

    inner = remote(
        orb.at[:, pl.ds(2 * (1 - core), DEPTH)], ext.at[:, pl.ds(14 * core, DEPTH)],
        s_in, r_in, twin,
    )
    outer, passed = [], []
    for n in range(PIECES):
        some = pl.ds(n * (ORB // PIECES), ORB // PIECES)
        outer.append(
            remote(
                orb.at[some, pl.ds(2 * core, DEPTH)], relay.at[some],
                s_out.at[n], r_relay.at[n], relayer,
            )
        )
        passed.append(
            remote(
                relay.at[some], ext.at[some, pl.ds(14 * core, DEPTH)],
                s_fwd.at[n], r_out.at[n], forward,
            )
        )

    locals_ = [
        pltpu.make_async_copy(orb, ext.at[:, pl.ds(DEPTH, PLANES)], l0.at[0]),
        pltpu.make_async_copy(pot, potv, l0.at[1]),
        pltpu.make_async_copy(
            earl.at[:, pl.ds(KEPT * band, KEPT)], rows.at[pl.ds(PREV * band, PREV)], l0.at[2]
        ),
        pltpu.make_async_copy(
            inc.at[:, pl.ds(KEPT * band, KEPT)],
            rows.at[pl.ds(2 * PREV + NEW * band, NEW)], l0.at[3],
        ),
    ]
    for copy in locals_:
        copy.start()
    inner.start()

    band_z[...] = band_matrix(CZ, CZ, -1.5 * coeffs[0])
    band_y[...] = band_matrix(PLANES * CY, CY, 0.0)
    for copy in locals_:
        copy.wait()

    def near(o, _):
        cells = ext[o, DEPTH : DEPTH + PLANES].reshape(PLANES * CY, CZ)
        field = potv[...].reshape(PLANES * CY, CZ)
        total = field * cells + nn(cells, band_z[...], HIGH) + nn(band_y[...], cells, HIGH)
        applied[o] = total.reshape(PLANES, CY, CZ)
        return 0

    grams[...] = jnp.zeros_like(grams)
    flat_rows = rows.reshape(ROWS * KEPT * CY, CZ)

    def take(k, _):
        for copy in give(k):
            copy.wait_recv()
        for copy in give(k):
            copy.wait_send()

        @pl.when(k + AHEAD < CHUNKS)
        def _():
            for copy in stage(k + AHEAD):
                copy.wait()
            for copy in give(k + AHEAD):
                copy.start()

        @pl.when(jnp.logical_and(k == 2, second))
        def _():
            pl.semaphore_wait(barrier, 11)
            tell(all_in)

        @pl.when(jnp.logical_and(k == 2, first))
        def _():
            pl.semaphore_wait(all_in, 1)

        @pl.when(jnp.logical_and(k == 2, early))
        def _():
            for copy in outer:
                copy.start()

        @pl.when(jnp.logical_and(k == CHUNKS - 1, jnp.logical_not(early)))
        def _():
            for copy in outer:
                copy.start()

        base = pl.multiple_of(k * CHUNK_Y, CHUNK_Y)
        for i in range(CHUNK_Y):
            hi, lo = split(flat_rows[pl.ds(base + i, ROWS, stride=KEPT * CY), :])
            at = pl.ds(pl.multiple_of((base + i) * CZ, CZ), CZ)
            high[:, at] = hi
            low[:, at] = lo
        at = pl.ds(pl.multiple_of(base * CZ, CHUNK_Y * CZ), CHUNK_Y * CZ)
        hi, lo = high[:, at], low[:, at]
        grams[...] += nt(hi, hi) + nt(hi, lo) + nt(lo, hi)

        @pl.when(k < CHUNKS - 1)
        def _():
            lax.fori_loop(k * NEAR, jnp.minimum((k + 1) * NEAR, ORB), near, 0)

        return 0

    lax.fori_loop(0, CHUNKS, take, 0)

    red[0:ROWS, :] = grams[:, 0 : 2 * PREV]
    red[ROWS:, :] = jnp.zeros((2 * NEW, 2 * PREV), F32)
    red[ROWS:, 0 : 2 * NEW] = grams[2 * PREV :, 2 * PREV :]

    sent = []
    def quarter(size, index):
        return pl.ds(pl.multiple_of(size * index, size), size)

    copies = [
        remote(
            red.at[quarter(64, (z + d) % 4)], got_z.at[d - 1],
            sz.at[d - 1], rz.at[d - 1], z_peers[d - 1],
        )
        for d in range(1, 4)
    ]
    for copy in copies:
        copy.start()
    for copy in copies:
        copy.wait_recv()
    sent = sent + copies
    sum_z[...] = red[quarter(64, z)] + got_z[0] + got_z[1] + got_z[2]
    copies = [
        remote(
            sum_z.at[quarter(16, (y + d) % 4)], got_y.at[d - 1],
            sy.at[d - 1], ry.at[d - 1], y_peers[d - 1],
        )
        for d in range(1, 4)
    ]
    for copy in copies:
        copy.start()
    for copy in copies:
        copy.wait_recv()
    sent = sent + copies
    part[...] = sum_z[quarter(16, y)] + got_y[0] + got_y[1] + got_y[2]
    to_twin = remote(part, twin_part, s_twin, r_twin, twin)
    along_x = [
        remote(
            pair, got_x.at[x], sx.at[2 * d + c], rx.at[d],
            device((x + d + 1) % 4, y, z, c),
        )
        for d in range(3)
        for c in range(2)
    ]
    back = remote(pair, got_x.at[x], sx.at[6], rx.at[3], twin)

    @pl.when(jnp.logical_not(early))
    def _():
        to_twin.start()

    @pl.when(early)
    def _():
        to_twin.wait_recv()
        pair[...] = part[...] + twin_part[...]
        for copy in along_x:
            copy.start()
        back.start()
        for n in range(PIECES):
            outer[n].wait_recv()
            passed[n].start()
        got_x[x] = pair[...]

    @pl.when(jnp.logical_not(early))
    def _():
        back.wait_recv()

    for copy in along_x[::2]:
        copy.wait_recv()
    total = got_x[0]
    for d in range(1, 4):
        total = total + got_x[d]
    whole_y[quarter(16, y)] = total * (1.0 / TOTAL)
    copies = [
        remote(
            whole_y.at[quarter(16, y)], whole_y.at[quarter(16, y)],
            sgy.at[d - 1], rgy.at[d - 1], y_peers[d - 1],
        )
        for d in range(1, 4)
    ]
    for copy in copies:
        copy.start()
    for copy in copies:
        copy.wait_recv()
    sent = sent + copies
    whole[quarter(64, z)] = whole_y[...]
    copies = [
        remote(
            whole_y, whole.at[quarter(64, z)], sgz.at[d - 1], rgz.at[d - 1], z_peers[d - 1]
        )
        for d in range(1, 4)
    ]
    for copy in copies:
        copy.start()
    for copy in copies:
        copy.wait_recv()
    sent = sent + copies

    corr_t = whole[2 * PREV : 2 * PREV + 2 * NEW]
    i = lax.broadcasted_iota(jnp.int32, (128, 128), 0)
    j = lax.broadcasted_iota(jnp.int32, (128, 128), 1)
    middle = whole[0 : 2 * PREV] - jnp.where(i == j, 2.0, 0.0)
    gram = whole[ROWS:, 0 : 2 * NEW] + nt(nn(corr_t, middle, HIGH), corr_t, HIGH)
    i = lax.broadcasted_iota(jnp.int32, (64, 128), 0)
    j = lax.broadcasted_iota(jnp.int32, (64, 128), 1)
    factor[...] = jnp.where(j == i + 64, 1.0, 0.0)
    factor[:, 0:64] = gram

    both = factor[...]
    for first in range(0, 64, 4):
        columns = [
            jnp.broadcast_to(both[:, first + n : first + n + 1], (64, 128)) for n in range(4)
        ]
        for n in range(4):
            step = first + n
            pivot = 1.0 / columns[n][step : step + 1]
            below = jnp.where(i > step, columns[n] * pivot, 0.0)
            both = both - below * both[step : step + 1]
            for m in range(n + 1, 4):
                columns[m] = columns[m] - below * columns[m][step : step + 1]
    pivots = jnp.sum(jnp.where(i == j, both, 0.0), axis=1, keepdims=True)
    root = lax.rsqrt(pivots)
    root = root * (1.5 - 0.5 * pivots * root * root)
    factor[...] = both * root
    inverse = factor[:, 64:128]
    inverse_hi, inverse_lo = split(inverse)
    corr_hi, corr_lo = split(corr_t)
    work[0:64] = -(
        nn(inverse_hi, corr_hi) + (nn(inverse_hi, corr_lo) + nn(inverse_lo, corr_hi))
    )
    theirs, own = pl.ds(NEW * other, NEW), pl.ds(NEW * band, NEW)
    prev_hi, prev_lo = split(jnp.concatenate([work[theirs], work[own]], axis=0))
    new_hi, new_lo = split(
        jnp.concatenate([factor[theirs, 64:128], factor[own, 64:128]], axis=0)
    )
    hi = jnp.concatenate([prev_hi, new_hi], axis=1)
    lo = jnp.concatenate([prev_lo, new_lo], axis=1)
    stacked = jnp.concatenate([hi, lo], axis=0)

    flat_outs = outs.reshape(NEW * KEPT * CY, CZ)
    flat_ortho = ortho.reshape(NEW * PLANES * CY, CZ)
    kept = pl.multiple_of(band * (KEPT * CY), KEPT * CY)

    def tile(k):
        return k // (CY // TILE_Y), pl.ds(
            pl.multiple_of((k % (CY // TILE_Y)) * TILE_Y, TILE_Y), TILE_Y
        )

    def send_new(k):
        plane, at = tile(k)
        return remote(
            outs.at[:, plane, at],
            ortho.at[:, KEPT * band + plane, at],
            s2.at[k], r2.at[k], partner,
        )

    def make(k, _):
        base = pl.multiple_of(k * TILE_Y, TILE_Y)
        at = pl.ds(pl.multiple_of(base * CZ, TILE_Y * CZ), TILE_Y * CZ)
        both = nn(stacked, high[:, at])
        total = both[0:64] + both[64:128] + nn(hi, low[:, at])
        for n in range(TILE_Y):
            at = slice(n * CZ, (n + 1) * CZ)
            flat_outs[pl.ds(base + n, NEW, stride=KEPT * CY), :] = total[:NEW, at]
            flat_ortho[pl.ds(kept + base + n, NEW, stride=PLANES * CY), :] = total[NEW:, at]
        send_new(k).start()

        @pl.when(jnp.logical_and(k == 3, jnp.logical_not(early)))
        def _():
            for n in range(PIECES):
                outer[n].wait_recv()
                passed[n].start()

        return 0

    lax.fori_loop(0, TILES, make, 0)

    work[...] = whole[2 * PREV :].T
    corr[...] = work[pl.ds(pl.multiple_of(PREV * band, PREV), PREV), 0 : 2 * NEW]

    inner.wait()
    for copy in passed:
        copy.wait_recv()

    def far(o, _):
        for p in range(PLANES):
            total = applied[o, p]
            for step in range(1, DEPTH + 1):
                total = total - (0.5 * coeffs[step]) * (
                    ext[o, p + DEPTH + step] + ext[o, p + DEPTH - step]
                )
            applied[o, p] = total
        return 0

    lax.fori_loop(0, ORB, far, 0)
    for copy in sent + outer + passed:
        copy.wait_send()

    @pl.when(early)
    def _():
        for copy in along_x + [back]:
            copy.wait_send()

    @pl.when(jnp.logical_not(early))
    def _():
        to_twin.wait_send()


    def finish(k, _):
        send_new(k).wait()
        return 0

    lax.fori_loop(0, TILES, finish, 0)


def hand_over(a, b, c, a_out, b_out, c_out, sems):
    copies = []
    for n in range(2):
        part = pl.ds(n * (ORB // 2), ORB // 2)
        copies.append(pltpu.make_async_copy(a.at[part], a_out.at[part], sems.at[n]))
    for n in range(4):
        part = pl.ds(n * (NEW // 4), NEW // 4)
        copies.append(pltpu.make_async_copy(c.at[part], c_out.at[part], sems.at[2 + n]))
    copies.append(pltpu.make_async_copy(b, b_out, sems.at[6]))
    for copy in copies:
        copy.start()
    for copy in copies:
        copy.wait()


def on_device(orbitals, potential, earlier, incoming):
    dma = pltpu.SemaphoreType.DMA
    any_ = pl.BlockSpec(memory_space=pl.ANY)
    shapes = (
        jax.ShapeDtypeStruct(orbitals.shape, F32),
        jax.ShapeDtypeStruct((PREV, 2 * NEW), F32),
        jax.ShapeDtypeStruct(incoming.shape, F32),
    )
    held = tuple(pltpu.VMEM(shape.shape, shape.dtype) for shape in shapes)
    in_vmem = pl.BlockSpec(memory_space=pltpu.VMEM)
    arguments = [
        pltpu.with_memory_space_constraint(a, pltpu.HBM)
        for a in (orbitals, potential, earlier, incoming)
    ]
    results = pl.pallas_call(
        kernel,
        out_shape=held,
        in_specs=[any_] * 4,
        out_specs=(in_vmem,) * 3,
        scratch_shapes=[
            pltpu.VMEM((PREV + NEW, KEPT, CY, CZ), F32),
            pltpu.VMEM((ROWS, KEPT, CY, CZ), F32),
            pltpu.VMEM((ROWS, CELLS), BF16),
            pltpu.VMEM((ROWS, CELLS), BF16),
            pltpu.VMEM((ORB, PLANES + 2 * DEPTH, CY, CZ), F32),
            pltpu.VMEM((PLANES, CY, CZ), F32),
            pltpu.VMEM((ORB, DEPTH, CY, CZ), F32),
            pltpu.VMEM((ROWS, ROWS), F32),
            pltpu.VMEM((256, 128), F32),
            pltpu.VMEM((3, 64, 128), F32),
            pltpu.VMEM((64, 128), F32),
            pltpu.VMEM((3, 16, 128), F32),
            pltpu.VMEM((16, 128), F32),
            pltpu.VMEM((16, 128), F32),
            pltpu.VMEM((16, 128), F32),
            pltpu.VMEM((4, 16, 128), F32),
            pltpu.VMEM((64, 128), F32),
            pltpu.VMEM((256, 128), F32),
            pltpu.VMEM((128, 128), F32),
            pltpu.VMEM((64, 128), F32),
            pltpu.VMEM((NEW, KEPT, CY, CZ), F32),
            pltpu.VMEM((CZ, CZ), F32),
            pltpu.VMEM((PLANES * CY, PLANES * CY), F32),
            dma((CHUNKS, 2)), dma((CHUNKS, 2)), dma((CHUNKS, 2)), dma((4,)),
            dma, dma, dma((PIECES,)), dma((PIECES,)), dma((PIECES,)), dma((PIECES,)),
            dma((3,)), dma((3,)), dma((3,)), dma((3,)), dma, dma, dma((7,)), dma((4,)),
            dma((3,)), dma((3,)), dma((3,)), dma((3,)),
            dma((TILES,)), dma((TILES,)),
            pltpu.SemaphoreType.REGULAR, pltpu.SemaphoreType.REGULAR,
        ],
        compiler_params=pltpu.CompilerParams(
            collective_id=0, has_side_effects=True, vmem_limit_bytes=50 * 2**20
        ),
        cost_estimate=pl.CostEstimate(
            flops=6 * 10**9, bytes_accessed=22 * 10**6, transcendentals=0
        ),
    )(*arguments)
    return pl.pallas_call(
        hand_over,
        out_shape=shapes,
        in_specs=[any_] * 3,
        out_specs=(any_,) * 3,
        scratch_shapes=[dma((7,))],
        compiler_params=pltpu.CompilerParams(vmem_limit_bytes=50 * 2**20),
        cost_estimate=pl.CostEstimate(flops=0, bytes_accessed=13 * 10**6, transcendentals=0),
    )(*[pltpu.with_memory_space_constraint(a, pltpu.VMEM) for a in results])


def solution(mesh):
    in_specs = (
        P("band", "domain", None, None),
        P("domain", None, None),
        P("band", "domain", None, None),
        P("band", "domain", None, None),
    )
    out_specs = (P("band", "domain", None, None), P("band", None), P("band", "domain", None, None))
    return jax.shard_map(
        on_device, mesh=mesh, in_specs=in_specs, out_specs=out_specs, check_vma=False
    )
```

time: 1090 us -> 227 us (0.21)
  blocking collectives: 643 us -> 0 us
  waiting for transfers between devices: 326 us -> 0 us
  Pallas kernels: 0 us -> 226 us
  matrix products: 51.4 us -> 0 us
  other arithmetic: 27.8 us -> 0 us
  local copies, waits for them, and re-layouts: 17.5 us -> 0 us
  between operations: 13.8 us -> 0.64 us
    psum x2 -> x0, blocking collectives: 643 us -> none  [the longest x1 323 us: on_device(): correlations = lax.psum(partial_correlations, 'domain')]
    pallas_call x0 -> x2, Pallas kernels: none -> 226 us  [the longest x1 223 us: on_device(): pl.pallas_call(kernel, out_shape=held, in_specs=[any_] * 4, out_specs=(in...]
    all_gather x2 -> x0, waiting for transfers between devices: 163 us -> none  [the longest x1 110 us: on_device(): gathered = lax.all_gather(mine_flat, 'band', axis=0, tiled=True)]
    reduce_scatter x1 -> x0, waiting for transfers between devices: 103 us -> none  [on_device(): lax.psum_scatter(jnp.dot(correlations.T, prev_flat, precision=high, prefe...]
    ppermute x2 -> x0, waiting for transfers between devices: 60.4 us -> none  [the longest x1 49.1 us: padded_2(): lax.ppermute(tail, axis, [(i, (i + 1) % count) for i in range(count)])]
    dot_general x4 -> x0, matrix products: 51.2 us -> none  [the longest x1 17.4 us: on_device(): jnp.dot(correlations.T, prev_flat, precision=high, preferred_element_type...]
    unnamed x9 -> x0, local copies, waits for them, and re-layouts: 13.7 us -> none
    another operation x5 -> x0, other arithmetic: 12.1 us -> none  [the longest x3 6.52 us: on_device(): factor = jnp.linalg.cholesky(gram)]
  transfers between devices with their start and end apart: 5 -> 0, of which waited for: 5 -> 0; matrix products, arithmetic and copies ran while one was open for 1% -> 0% of each run, Pallas kernels for 0% -> 0%
where the time goes in v1:
time: 227 us; the launch traced here: 226 us
  Pallas kernels  226 us (100%)
    pallas_call x1, Pallas kernels, on_device(): pl.pallas_call(kernel, out_shape=held, in_specs=[any_] * 4, out_specs=(in...  223 us

profile of v1, /device:TPU:1, one launch (start us, length us, event | category | flops | bytes accessed | tf_op | source)
XLA Modules:
  0.0 226.5 jit_solution(3229341274552839582)
XLA Ops:
  0.6 223.1 %shard_map.67 = (f32[16,8,32,128]{3,2,1,0:T(8,128)S(1)}, f32[64,64]{1,0:T(8,128)S(1)}, f32[32,8,32,128]{3,2,1,0:T(8,128)S(1)}) custom-call(f32[16,8,32,128]{3,2,1,0:T(8,128)} %orb.1, f32[8,32,128]{2,1,0:T(8,128)} %pot.1, f32[64,8,32,128]{3,2,1,0:T(8,128)} %earl.1, f32[32,8,32,128]{3,2,1,0:T(8,128)} %inc.1), custom_call_target="tpu_custom_call" | custom-call | flops 6000000000 | bytes 22000000 | tf_op jit(solution)/shard_map/pallas_call | solution.py:546
  223.8 2.7 %shard_map.68 = (f32[16,8,32,128]{3,2,1,0:T(8,128)}, f32[64,64]{1,0:T(8,128)}, f32[32,8,32,128]{3,2,1,0:T(8,128)}) custom-call(f32[16,8,32,128]{3,2,1,0:T(8,128)S(1)} %get-tuple-element.6.a, f32[64,64]{1,0:T(8,128)S(1)} %get-tuple-element.7.b, f32[32,8,32,128]{3,2,1,0:T(8,128)S(1)} %get-tuple-element.8.c), custom_call_target="tpu_custom_call" | custom-call | bytes 13000000 | tf_op jit(solution)/shard_map/pallas_call | solution.py:589

commit v2 on v1

--- a/solution.py
+++ b/solution.py
@@ -29,6 +29,13 @@
 CZ = 128
 DEPTH = 6
 ROWS = 2 * PREV + 2 * NEW
+HALF_ROWS = PREV + NEW
+ORDER = (
+    (0, PREV, 0),
+    (HALF_ROWS, PREV, PREV),
+    (PREV, NEW, 2 * PREV),
+    (HALF_ROWS + PREV, NEW, 2 * PREV + NEW),
+)
 CELLS = KEPT * CY * CZ
 TOTAL = 512 * CY * CZ
 
@@ -75,7 +82,7 @@
     applied, corr, ortho,
     to_give, rows, high, low, ext, potv, relay, grams, red,
     got_z, sum_z, got_y, part, twin_part, pair, got_x, whole_y, whole, work, factor, outs, band_z, band_y,
-    s1, r1, l1, l0,
+    s1, r1, l1, l2, l0,
     s_in, r_in, s_out, r_relay, s_fwd, r_out,
     sz, rz, sy, ry, s_twin, r_twin, sx, rx, sgy, rgy, sgz, rgz,
     s2, r2, go, all_in,
@@ -116,25 +123,32 @@
     chip_giver = (other, giver_domain - giver_domain % 2 + 1)
     early = early == 1
 
-    def piece(k):
-        plane = k // (CY // CHUNK_Y)
-        return plane, pl.ds(pl.multiple_of((k % (CY // CHUNK_Y)) * CHUNK_Y, CHUNK_Y), CHUNK_Y)
+    def piece(planes, k):
+        plane = planes + k // (CY // CHUNK_Y)
+        at = pl.multiple_of((k % (CY // CHUNK_Y)) * CHUNK_Y, CHUNK_Y)
+        return plane, pl.ds(at, CHUNK_Y)
 
     def stage(k):
-        plane, at = piece(k)
+        plane, at = piece(KEPT * other, k)
+        return (
+            pltpu.make_async_copy(earl.at[:, plane, at], to_give.at[k, 0:PREV], l1.at[k, 0]),
+            pltpu.make_async_copy(inc.at[:, plane, at], to_give.at[k, PREV:], l1.at[k, 1]),
+        )
+
+    def own(k):
+        plane, at = piece(KEPT * band, k)
         return (
             pltpu.make_async_copy(
-                earl.at[:, KEPT * other + plane, at], to_give.at[0:PREV, plane, at], l1.at[k, 0]
+                earl.at[:, plane, at], rows.at[k, pl.ds(HALF_ROWS * band, PREV)], l2.at[k, 0]
             ),
             pltpu.make_async_copy(
-                inc.at[:, KEPT * other + plane, at], to_give.at[PREV:, plane, at], l1.at[k, 1]
+                inc.at[:, plane, at], rows.at[k, pl.ds(HALF_ROWS * band + PREV, NEW)], l2.at[k, 1]
             ),
         )
 
-    def stage_all(k, _):
+    for k in range(AHEAD):
         for copy in stage(k):
             copy.start()
-        return 0
 
     barrier = pltpu.get_barrier_semaphore()
     first, second = core == 0, core == 1
@@ -153,8 +167,6 @@
     @pl.when(first)
     def _():
         greet(partner)
-
-    lax.fori_loop(0, CHUNKS, stage_all, 0)
 
     @pl.when(first)
     def _():
@@ -172,25 +184,26 @@
         )
 
     def give(k):
-        plane, at = piece(k)
-        return (
-            remote(
-                to_give.at[0:PREV, plane, at],
-                rows.at[pl.ds(PREV * band, PREV), plane, at],
-                s1.at[k, 0], r1.at[k, 0], partner,
-            ),
-            remote(
-                to_give.at[PREV:, plane, at],
-                rows.at[pl.ds(2 * PREV + NEW * band, NEW), plane, at],
-                s1.at[k, 1], r1.at[k, 1], partner,
-            ),
+        return remote(
+            to_give.at[k], rows.at[k, pl.ds(HALF_ROWS * band, HALF_ROWS)],
+            s1.at[k], r1.at[k], partner,
         )
 
     for k in range(AHEAD):
         for copy in stage(k):
             copy.wait()
-        for copy in give(k):
+        give(k).start()
+
+    def fetch(k, _):
+        for copy in own(k):
             copy.start()
+
+        @pl.when(k + AHEAD < CHUNKS)
+        def _():
+            for copy in stage(k + AHEAD):
+                copy.start()
+
+        return 0
 
     @pl.when(second)
     def _():
@@ -224,16 +237,10 @@
     locals_ = [
         pltpu.make_async_copy(orb, ext.at[:, pl.ds(DEPTH, PLANES)], l0.at[0]),
         pltpu.make_async_copy(pot, potv, l0.at[1]),
-        pltpu.make_async_copy(
-            earl.at[:, pl.ds(KEPT * band, KEPT)], rows.at[pl.ds(PREV * band, PREV)], l0.at[2]
-        ),
-        pltpu.make_async_copy(
-            inc.at[:, pl.ds(KEPT * band, KEPT)],
-            rows.at[pl.ds(2 * PREV + NEW * band, NEW)], l0.at[3],
-        ),
     ]
     for copy in locals_:
         copy.start()
+    lax.fori_loop(0, CHUNKS, fetch, 0)
     inner.start()
 
     band_z[...] = band_matrix(CZ, CZ, -1.5 * coeffs[0])
@@ -249,20 +256,20 @@
         return 0
 
     grams[...] = jnp.zeros_like(grams)
-    flat_rows = rows.reshape(ROWS * KEPT * CY, CZ)
+    flat_rows = rows.reshape(CHUNKS * ROWS * CHUNK_Y, CZ)
 
     def take(k, _):
-        for copy in give(k):
-            copy.wait_recv()
-        for copy in give(k):
-            copy.wait_send()
+        give(k).wait_recv()
+        give(k).wait_send()
 
         @pl.when(k + AHEAD < CHUNKS)
         def _():
             for copy in stage(k + AHEAD):
                 copy.wait()
-            for copy in give(k + AHEAD):
-                copy.start()
+            give(k + AHEAD).start()
+
+        for copy in own(k):
+            copy.wait()
 
         @pl.when(jnp.logical_and(k == 2, second))
         def _():
@@ -284,11 +291,15 @@
                 copy.start()
 
         base = pl.multiple_of(k * CHUNK_Y, CHUNK_Y)
+        start = pl.multiple_of(k * (ROWS * CHUNK_Y), ROWS * CHUNK_Y)
         for i in range(CHUNK_Y):
-            hi, lo = split(flat_rows[pl.ds(base + i, ROWS, stride=KEPT * CY), :])
             at = pl.ds(pl.multiple_of((base + i) * CZ, CZ), CZ)
-            high[:, at] = hi
-            low[:, at] = lo
+            for row, count, to in ORDER:
+                hi, lo = split(
+                    flat_rows[pl.ds(start + row * CHUNK_Y + i, count, stride=CHUNK_Y), :]
+                )
+                high[to : to + count, at] = hi
+                low[to : to + count, at] = lo
         at = pl.ds(pl.multiple_of(base * CZ, CHUNK_Y * CZ), CHUNK_Y * CZ)
         hi, lo = high[:, at], low[:, at]
         grams[...] += nt(hi, hi) + nt(hi, lo) + nt(lo, hi)
@@ -549,8 +560,8 @@
         in_specs=[any_] * 4,
         out_specs=(in_vmem,) * 3,
         scratch_shapes=[
-            pltpu.VMEM((PREV + NEW, KEPT, CY, CZ), F32),
-            pltpu.VMEM((ROWS, KEPT, CY, CZ), F32),
+            pltpu.VMEM((CHUNKS, HALF_ROWS, CHUNK_Y, CZ), F32),
+            pltpu.VMEM((CHUNKS, ROWS, CHUNK_Y, CZ), F32),
             pltpu.VMEM((ROWS, CELLS), BF16),
             pltpu.VMEM((ROWS, CELLS), BF16),
             pltpu.VMEM((ORB, PLANES + 2 * DEPTH, CY, CZ), F32),
@@ -572,7 +583,7 @@
             pltpu.VMEM((NEW, KEPT, CY, CZ), F32),
             pltpu.VMEM((CZ, CZ), F32),
             pltpu.VMEM((PLANES * CY, PLANES * CY), F32),
-            dma((CHUNKS, 2)), dma((CHUNKS, 2)), dma((CHUNKS, 2)), dma((4,)),
+            dma((CHUNKS,)), dma((CHUNKS,)), dma((CHUNKS, 2)), dma((CHUNKS, 2)), dma((2,)),
             dma, dma, dma((PIECES,)), dma((PIECES,)), dma((PIECES,)), dma((PIECES,)),
             dma((3,)), dma((3,)), dma((3,)), dma((3,)), dma, dma, dma((7,)), dma((4,)),
             dma((3,)), dma((3,)), dma((3,)), dma((3,)),

time: 227 us -> 227 us (level)
  no operation moved by 1% of the time
where the time goes in v2:
time: 227 us; the launch traced here: 226 us
  Pallas kernels  226 us (100%)
    pallas_call x1, Pallas kernels, on_device(): pl.pallas_call(kernel, out_shape=held, in_specs=[any_] * 4, out_specs=(in...  223 us

profile of v2, /device:TPU:1, one launch (start us, length us, event | category | flops | bytes accessed | tf_op | source)
XLA Modules:
  0.0 226.5 jit_solution(13271583532827163465)
XLA Ops:
  0.6 223.1 %shard_map.67 = (f32[16,8,32,128]{3,2,1,0:T(8,128)S(1)}, f32[64,64]{1,0:T(8,128)S(1)}, f32[32,8,32,128]{3,2,1,0:T(8,128)S(1)}) custom-call(f32[16,8,32,128]{3,2,1,0:T(8,128)} %orb.1, f32[8,32,128]{2,1,0:T(8,128)} %pot.1, f32[64,8,32,128]{3,2,1,0:T(8,128)} %earl.1, f32[32,8,32,128]{3,2,1,0:T(8,128)} %inc.1), custom_call_target="tpu_custom_call" | custom-call | flops 6000000000 | bytes 22000000 | tf_op jit(solution)/shard_map/pallas_call | solution.py:557
  223.7 2.7 %shard_map.68 = (f32[16,8,32,128]{3,2,1,0:T(8,128)}, f32[64,64]{1,0:T(8,128)}, f32[32,8,32,128]{3,2,1,0:T(8,128)}) custom-call(f32[16,8,32,128]{3,2,1,0:T(8,128)S(1)} %get-tuple-element.6.a, f32[64,64]{1,0:T(8,128)S(1)} %get-tuple-element.7.b, f32[32,8,32,128]{3,2,1,0:T(8,128)S(1)} %get-tuple-element.8.c), custom_call_target="tpu_custom_call" | custom-call | bytes 13000000 | tf_op jit(solution)/shard_map/pallas_call | solution.py:600

commit v3 on v2

--- a/solution.py
+++ b/solution.py
@@ -117,10 +117,10 @@
     to = (chip + x // 2) * 2 + band + way + 64
     to = to % 64
     chip_passer = device(
-        (((to // 2) % 2) * 2 + band - way + 4) % 4, (to // 4) % 4, to // 16, 1
+        (((to // 2) % 2) * 2 + band - way + 4) % 4, (to // 4) % 4, to // 16, 0
     )
     giver_domain = ((chip + ((x - way + 4) % 4) // 2) * 2 + band + way + 64) % 64
-    chip_giver = (other, giver_domain - giver_domain % 2 + 1)
+    chip_giver = (other, giver_domain - giver_domain % 2)
     early = early == 1
 
     def piece(planes, k):
@@ -151,7 +151,7 @@
             copy.start()
 
     barrier = pltpu.get_barrier_semaphore()
-    first, second = core == 0, core == 1
+    first, second = core == 1, core == 0
 
     def greet(peer):
         pl.semaphore_signal(barrier, inc=1, device_id=peer, device_id_type=MESH)
@@ -162,7 +162,7 @@
     @pl.when(second)
     def _():
         greet(twin)
-        greet((other, domain - 1))
+        greet((other, domain + 1))
 
     @pl.when(first)
     def _():
@@ -208,9 +208,9 @@
     @pl.when(second)
     def _():
         for d in range(1, 4):
-            greet(device(x, y, (z + d) % 4, 1))
-            greet(device(x, (y + d) % 4, z, 1))
-            greet(device((x + d) % 4, y, z, 1))
+            greet(device(x, y, (z + d) % 4, 0))
+            greet(device(x, (y + d) % 4, z, 0))
+            greet(device((x + d) % 4, y, z, 0))
         greet(chip_passer)
         greet(chip_giver)
 

time: 227 us -> 226 us (level)
  no operation moved by 1% of the time
where the time goes in v3:
time: 226 us
  Pallas kernels  225 us (100%)
    pallas_call x1, Pallas kernels, on_device(): pl.pallas_call(kernel, out_shape=held, in_specs=[any_] * 4, out_specs=(in...  223 us

profile of v3, /device:TPU:1, one launch (start us, length us, event | category | flops | bytes accessed | tf_op | source)
XLA Modules:
  0.0 226.1 jit_solution(11478722484026001914)
XLA Ops:
  0.6 222.7 %shard_map.67 = (f32[16,8,32,128]{3,2,1,0:T(8,128)S(1)}, f32[64,64]{1,0:T(8,128)S(1)}, f32[32,8,32,128]{3,2,1,0:T(8,128)S(1)}) custom-call(f32[16,8,32,128]{3,2,1,0:T(8,128)} %orb.1, f32[8,32,128]{2,1,0:T(8,128)} %pot.1, f32[64,8,32,128]{3,2,1,0:T(8,128)} %earl.1, f32[32,8,32,128]{3,2,1,0:T(8,128)} %inc.1), custom_call_target="tpu_custom_call" | custom-call | flops 6000000000 | bytes 22000000 | tf_op jit(solution)/shard_map/pallas_call | solution.py:557
  223.4 2.7 %shard_map.68 = (f32[16,8,32,128]{3,2,1,0:T(8,128)}, f32[64,64]{1,0:T(8,128)}, f32[32,8,32,128]{3,2,1,0:T(8,128)}) custom-call(f32[16,8,32,128]{3,2,1,0:T(8,128)S(1)} %get-tuple-element.6.a, f32[64,64]{1,0:T(8,128)S(1)} %get-tuple-element.7.b, f32[32,8,32,128]{3,2,1,0:T(8,128)S(1)} %get-tuple-element.8.c), custom_call_target="tpu_custom_call" | custom-call | bytes 13000000 | tf_op jit(solution)/shard_map/pallas_call | solution.py:600

commit v4 on v2

--- a/solution.py
+++ b/solution.py
@@ -45,6 +45,7 @@
 NEAR = -(-ORB // (CHUNKS - 1))
 PIECES = 2
 TILES = 16
+LAG = 2
 TILE_Y = KEPT * CY // TILES
 
 
@@ -475,7 +476,11 @@
             at = slice(n * CZ, (n + 1) * CZ)
             flat_outs[pl.ds(base + n, NEW, stride=KEPT * CY), :] = total[:NEW, at]
             flat_ortho[pl.ds(kept + base + n, NEW, stride=PLANES * CY), :] = total[NEW:, at]
-        send_new(k).start()
+        ready = k - LAG * (1 - core)
+
+        @pl.when(ready >= 0)
+        def _():
+            send_new(ready).start()
 
         @pl.when(jnp.logical_and(k == 3, jnp.logical_not(early)))
         def _():
@@ -486,6 +491,12 @@
         return 0
 
     lax.fori_loop(0, TILES, make, 0)
+
+    @pl.when(core == 0)
+    def _():
+        for k in range(TILES - LAG, TILES):
+            send_new(k).start()
+
 
     work[...] = whole[2 * PREV :].T
     corr[...] = work[pl.ds(pl.multiple_of(PREV * band, PREV), PREV), 0 : 2 * NEW]

time: 227 us -> 227 us (level)
  no operation moved by 1% of the time
where the time goes in v4:
time: 227 us; the launch traced here: 226 us
  Pallas kernels  226 us (100%)
    pallas_call x1, Pallas kernels, on_device(): pl.pallas_call(kernel, out_shape=held, in_specs=[any_] * 4, out_specs=(in...  223 us

profile of v4, /device:TPU:1, one launch (start us, length us, event | category | flops | bytes accessed | tf_op | source)
XLA Modules:
  0.0 226.5 jit_solution(17228575156976861611)
XLA Ops:
  0.6 223.1 %shard_map.67 = (f32[16,8,32,128]{3,2,1,0:T(8,128)S(1)}, f32[64,64]{1,0:T(8,128)S(1)}, f32[32,8,32,128]{3,2,1,0:T(8,128)S(1)}) custom-call(f32[16,8,32,128]{3,2,1,0:T(8,128)} %orb.1, f32[8,32,128]{2,1,0:T(8,128)} %pot.1, f32[64,8,32,128]{3,2,1,0:T(8,128)} %earl.1, f32[32,8,32,128]{3,2,1,0:T(8,128)} %inc.1), custom_call_target="tpu_custom_call" | custom-call | flops 6000000000 | bytes 22000000 | tf_op jit(solution)/shard_map/pallas_call | solution.py:568
  223.7 2.7 %shard_map.68 = (f32[16,8,32,128]{3,2,1,0:T(8,128)}, f32[64,64]{1,0:T(8,128)}, f32[32,8,32,128]{3,2,1,0:T(8,128)}) custom-call(f32[16,8,32,128]{3,2,1,0:T(8,128)S(1)} %get-tuple-element.6.a, f32[64,64]{1,0:T(8,128)S(1)} %get-tuple-element.7.b, f32[32,8,32,128]{3,2,1,0:T(8,128)S(1)} %get-tuple-element.8.c), custom_call_target="tpu_custom_call" | custom-call | bytes 13000000 | tf_op jit(solution)/shard_map/pallas_call | solution.py:611

commit v5 on v2

--- a/solution.py
+++ b/solution.py
@@ -43,7 +43,7 @@
 CHUNK_Y = KEPT * CY // CHUNKS
 AHEAD = 2
 NEAR = -(-ORB // (CHUNKS - 1))
-PIECES = 2
+PIECES = 4
 TILES = 16
 TILE_Y = KEPT * CY // TILES
 
@@ -290,6 +290,11 @@
             for copy in outer:
                 copy.start()
 
+        @pl.when(jnp.logical_and(k == CHUNKS - 1, early))
+        def _():
+            outer[0].wait_recv()
+            passed[0].start()
+
         base = pl.multiple_of(k * CHUNK_Y, CHUNK_Y)
         start = pl.multiple_of(k * (ROWS * CHUNK_Y), ROWS * CHUNK_Y)
         for i in range(CHUNK_Y):
@@ -368,7 +373,7 @@
         for copy in along_x:
             copy.start()
         back.start()
-        for n in range(PIECES):
+        for n in range(1, PIECES):
             outer[n].wait_recv()
             passed[n].start()
         got_x[x] = pair[...]

time: 227 us -> 226 us (level)
  no operation moved by 1% of the time
where the time goes in v5:
time: 226 us
  Pallas kernels  225 us (100%)
    pallas_call x1, Pallas kernels, on_device(): pl.pallas_call(kernel, out_shape=held, in_specs=[any_] * 4, out_specs=(in...  222 us

profile of v5, /device:TPU:1, one launch (start us, length us, event | category | flops | bytes accessed | tf_op | source)
XLA Modules:
  0.0 225.6 jit_solution(9913173079542318108)
XLA Ops:
  0.6 222.2 %shard_map.67 = (f32[16,8,32,128]{3,2,1,0:T(8,128)S(1)}, f32[64,64]{1,0:T(8,128)S(1)}, f32[32,8,32,128]{3,2,1,0:T(8,128)S(1)}) custom-call(f32[16,8,32,128]{3,2,1,0:T(8,128)} %orb.1, f32[8,32,128]{2,1,0:T(8,128)} %pot.1, f32[64,8,32,128]{3,2,1,0:T(8,128)} %earl.1, f32[32,8,32,128]{3,2,1,0:T(8,128)} %inc.1), custom_call_target="tpu_custom_call" | custom-call | flops 6000000000 | bytes 22000000 | tf_op jit(solution)/shard_map/pallas_call | solution.py:562
  222.8 2.7 %shard_map.68 = (f32[16,8,32,128]{3,2,1,0:T(8,128)}, f32[64,64]{1,0:T(8,128)}, f32[32,8,32,128]{3,2,1,0:T(8,128)}) custom-call(f32[16,8,32,128]{3,2,1,0:T(8,128)S(1)} %get-tuple-element.6.a, f32[64,64]{1,0:T(8,128)S(1)} %get-tuple-element.7.b, f32[32,8,32,128]{3,2,1,0:T(8,128)S(1)} %get-tuple-element.8.c), custom_call_target="tpu_custom_call" | custom-call | bytes 13000000 | tf_op jit(solution)/shard_map/pallas_call | solution.py:605

commit v6 on v5

--- a/solution.py
+++ b/solution.py
@@ -285,11 +285,6 @@
             for copy in outer:
                 copy.start()
 
-        @pl.when(jnp.logical_and(k == CHUNKS - 1, jnp.logical_not(early)))
-        def _():
-            for copy in outer:
-                copy.start()
-
         @pl.when(jnp.logical_and(k == CHUNKS - 1, early))
         def _():
             outer[0].wait_recv()
@@ -308,6 +303,11 @@
         at = pl.ds(pl.multiple_of(base * CZ, CHUNK_Y * CZ), CHUNK_Y * CZ)
         hi, lo = high[:, at], low[:, at]
         grams[...] += nt(hi, hi) + nt(hi, lo) + nt(lo, hi)
+
+        @pl.when(jnp.logical_and(k == CHUNKS - 2, jnp.logical_not(early)))
+        def _():
+            for copy in outer:
+                copy.start()
 
         @pl.when(k < CHUNKS - 1)
         def _():

time: 226 us -> 223 us (0.987)
    pallas_call x1, Pallas kernels: 222 us -> 220 us  [on_device(): pl.pallas_call(kernel, out_shape=held, in_specs=[any_] * 4, out_specs=(in...]
where the time goes in v6:
time: 223 us
  Pallas kernels  223 us (100%)
    pallas_call x1, Pallas kernels, on_device(): pl.pallas_call(kernel, out_shape=held, in_specs=[any_] * 4, out_specs=(in...  220 us

profile of v6, /device:TPU:1, one launch (start us, length us, event | category | flops | bytes accessed | tf_op | source)
XLA Modules:
  0.0 223.2 jit_solution(8575980772726880973)
XLA Ops:
  0.6 219.8 %shard_map.67 = (f32[16,8,32,128]{3,2,1,0:T(8,128)S(1)}, f32[64,64]{1,0:T(8,128)S(1)}, f32[32,8,32,128]{3,2,1,0:T(8,128)S(1)}) custom-call(f32[16,8,32,128]{3,2,1,0:T(8,128)} %orb.1, f32[8,32,128]{2,1,0:T(8,128)} %pot.1, f32[64,8,32,128]{3,2,1,0:T(8,128)} %earl.1, f32[32,8,32,128]{3,2,1,0:T(8,128)} %inc.1), custom_call_target="tpu_custom_call" | custom-call | flops 6000000000 | bytes 22000000 | tf_op jit(solution)/shard_map/pallas_call | solution.py:562
  220.5 2.7 %shard_map.68 = (f32[16,8,32,128]{3,2,1,0:T(8,128)}, f32[64,64]{1,0:T(8,128)}, f32[32,8,32,128]{3,2,1,0:T(8,128)}) custom-call(f32[16,8,32,128]{3,2,1,0:T(8,128)S(1)} %get-tuple-element.6.a, f32[64,64]{1,0:T(8,128)S(1)} %get-tuple-element.7.b, f32[32,8,32,128]{3,2,1,0:T(8,128)S(1)} %get-tuple-element.8.c), custom_call_target="tpu_custom_call" | custom-call | bytes 13000000 | tf_op jit(solution)/shard_map/pallas_call | solution.py:605

commit v7 on v6

--- a/solution.py
+++ b/solution.py
@@ -30,12 +30,6 @@
 DEPTH = 6
 ROWS = 2 * PREV + 2 * NEW
 HALF_ROWS = PREV + NEW
-ORDER = (
-    (0, PREV, 0),
-    (HALF_ROWS, PREV, PREV),
-    (PREV, NEW, 2 * PREV),
-    (HALF_ROWS + PREV, NEW, 2 * PREV + NEW),
-)
 CELLS = KEPT * CY * CZ
 TOTAL = 512 * CY * CZ
 
@@ -258,6 +252,27 @@
     grams[...] = jnp.zeros_like(grams)
     flat_rows = rows.reshape(CHUNKS * ROWS * CHUNK_Y, CZ)
 
+    def spread(k, side):
+        base = pl.multiple_of(k * CHUNK_Y, CHUNK_Y)
+        start = pl.multiple_of((k * 2 + side) * (HALF_ROWS * CHUNK_Y), HALF_ROWS * CHUNK_Y)
+        places = ((0, PREV, PREV * side), (PREV, NEW, 2 * PREV + NEW * side))
+        for i in range(CHUNK_Y):
+            at = pl.ds(pl.multiple_of((base + i) * CZ, CZ), CZ)
+            for row, count, to in places:
+                hi, lo = split(
+                    flat_rows[pl.ds(start + row * CHUNK_Y + i, count, stride=CHUNK_Y), :]
+                )
+                to = pl.ds(pl.multiple_of(to, NEW), count)
+                high[to, at] = hi
+                low[to, at] = lo
+
+    def spread_own(k):
+        for copy in own(k):
+            copy.wait()
+        spread(k, band)
+
+    spread_own(0)
+
     def take(k, _):
         give(k).wait_recv()
         give(k).wait_send()
@@ -268,9 +283,6 @@
                 copy.wait()
             give(k + AHEAD).start()
 
-        for copy in own(k):
-            copy.wait()
-
         @pl.when(jnp.logical_and(k == 2, second))
         def _():
             pl.semaphore_wait(barrier, 11)
@@ -291,15 +303,7 @@
             passed[0].start()
 
         base = pl.multiple_of(k * CHUNK_Y, CHUNK_Y)
-        start = pl.multiple_of(k * (ROWS * CHUNK_Y), ROWS * CHUNK_Y)
-        for i in range(CHUNK_Y):
-            at = pl.ds(pl.multiple_of((base + i) * CZ, CZ), CZ)
-            for row, count, to in ORDER:
-                hi, lo = split(
-                    flat_rows[pl.ds(start + row * CHUNK_Y + i, count, stride=CHUNK_Y), :]
-                )
-                high[to : to + count, at] = hi
-                low[to : to + count, at] = lo
+        spread(k, other)
         at = pl.ds(pl.multiple_of(base * CZ, CHUNK_Y * CZ), CHUNK_Y * CZ)
         hi, lo = high[:, at], low[:, at]
         grams[...] += nt(hi, hi) + nt(hi, lo) + nt(lo, hi)
@@ -311,6 +315,7 @@
 
         @pl.when(k < CHUNKS - 1)
         def _():
+            spread_own(k + 1)
             lax.fori_loop(k * NEAR, jnp.minimum((k + 1) * NEAR, ORB), near, 0)
 
         return 0

time: 223 us -> 223 us (level)
  no operation moved by 1% of the time
where the time goes in v7:
time: 223 us
  Pallas kernels  223 us (100%)
    pallas_call x1, Pallas kernels, on_device(): pl.pallas_call(kernel, out_shape=held, in_specs=[any_] * 4, out_specs=(in...  220 us

profile of v7, /device:TPU:1, one launch (start us, length us, event | category | flops | bytes accessed | tf_op | source)
XLA Modules:
  0.0 223.2 jit_solution(6880201624032670568)
XLA Ops:
  0.6 219.8 %shard_map.67 = (f32[16,8,32,128]{3,2,1,0:T(8,128)S(1)}, f32[64,64]{1,0:T(8,128)S(1)}, f32[32,8,32,128]{3,2,1,0:T(8,128)S(1)}) custom-call(f32[16,8,32,128]{3,2,1,0:T(8,128)} %orb.1, f32[8,32,128]{2,1,0:T(8,128)} %pot.1, f32[64,8,32,128]{3,2,1,0:T(8,128)} %earl.1, f32[32,8,32,128]{3,2,1,0:T(8,128)} %inc.1), custom_call_target="tpu_custom_call" | custom-call | flops 6000000000 | bytes 22000000 | tf_op jit(solution)/shard_map/pallas_call | solution.py:567
  220.5 2.7 %shard_map.68 = (f32[16,8,32,128]{3,2,1,0:T(8,128)}, f32[64,64]{1,0:T(8,128)}, f32[32,8,32,128]{3,2,1,0:T(8,128)}) custom-call(f32[16,8,32,128]{3,2,1,0:T(8,128)S(1)} %get-tuple-element.6.a, f32[64,64]{1,0:T(8,128)S(1)} %get-tuple-element.7.b, f32[32,8,32,128]{3,2,1,0:T(8,128)S(1)} %get-tuple-element.8.c), custom_call_target="tpu_custom_call" | custom-call | bytes 13000000 | tf_op jit(solution)/shard_map/pallas_call | solution.py:610

commit v8 on v6

--- a/solution.py
+++ b/solution.py
@@ -285,11 +285,6 @@
             for copy in outer:
                 copy.start()
 
-        @pl.when(jnp.logical_and(k == CHUNKS - 1, early))
-        def _():
-            outer[0].wait_recv()
-            passed[0].start()
-
         base = pl.multiple_of(k * CHUNK_Y, CHUNK_Y)
         start = pl.multiple_of(k * (ROWS * CHUNK_Y), ROWS * CHUNK_Y)
         for i in range(CHUNK_Y):
@@ -308,6 +303,11 @@
         def _():
             for copy in outer:
                 copy.start()
+
+        @pl.when(jnp.logical_and(k == CHUNKS - 2, early))
+        def _():
+            outer[0].wait_recv()
+            passed[0].start()
 
         @pl.when(k < CHUNKS - 1)
         def _():

time: 223 us -> 223 us (level)
  no operation moved by 1% of the time
where the time goes in v8:
time: 223 us
  Pallas kernels  223 us (100%)
    pallas_call x1, Pallas kernels, on_device(): pl.pallas_call(kernel, out_shape=held, in_specs=[any_] * 4, out_specs=(in...  220 us

profile of v8, /device:TPU:1, one launch (start us, length us, event | category | flops | bytes accessed | tf_op | source)
XLA Modules:
  0.0 223.2 jit_solution(333420950819884136)
XLA Ops:
  0.6 219.8 %shard_map.67 = (f32[16,8,32,128]{3,2,1,0:T(8,128)S(1)}, f32[64,64]{1,0:T(8,128)S(1)}, f32[32,8,32,128]{3,2,1,0:T(8,128)S(1)}) custom-call(f32[16,8,32,128]{3,2,1,0:T(8,128)} %orb.1, f32[8,32,128]{2,1,0:T(8,128)} %pot.1, f32[64,8,32,128]{3,2,1,0:T(8,128)} %earl.1, f32[32,8,32,128]{3,2,1,0:T(8,128)} %inc.1), custom_call_target="tpu_custom_call" | custom-call | flops 6000000000 | bytes 22000000 | tf_op jit(solution)/shard_map/pallas_call | solution.py:562
  220.5 2.7 %shard_map.68 = (f32[16,8,32,128]{3,2,1,0:T(8,128)}, f32[64,64]{1,0:T(8,128)}, f32[32,8,32,128]{3,2,1,0:T(8,128)}) custom-call(f32[16,8,32,128]{3,2,1,0:T(8,128)S(1)} %get-tuple-element.6.a, f32[64,64]{1,0:T(8,128)S(1)} %get-tuple-element.7.b, f32[32,8,32,128]{3,2,1,0:T(8,128)S(1)} %get-tuple-element.8.c), custom_call_target="tpu_custom_call" | custom-call | bytes 13000000 | tf_op jit(solution)/shard_map/pallas_call | solution.py:605

commit v9 on v6

--- a/solution.py
+++ b/solution.py
@@ -90,18 +90,101 @@
     band = lax.axis_index("band")
     domain = lax.axis_index("domain")
     core = domain % 2
+    other = 1 - band
+    partner = (other, domain)
+    twin = (band, domain + 1 - 2 * core)
+
+    def piece(planes, k):
+        plane = planes + k // (CY // CHUNK_Y)
+        at = pl.multiple_of((k % (CY // CHUNK_Y)) * CHUNK_Y, CHUNK_Y)
+        return plane, pl.ds(at, CHUNK_Y)
+
+    def stage(k):
+        plane, at = piece(KEPT * other, k)
+        return (
+            pltpu.make_async_copy(earl.at[:, plane, at], to_give.at[k, 0:PREV], l1.at[k, 0]),
+            pltpu.make_async_copy(inc.at[:, plane, at], to_give.at[k, PREV:], l1.at[k, 1]),
+        )
+
+    def own(k):
+        plane, at = piece(KEPT * band, k)
+        return (
+            pltpu.make_async_copy(
+                earl.at[:, plane, at], rows.at[k, pl.ds(HALF_ROWS * band, PREV)], l2.at[k, 0]
+            ),
+            pltpu.make_async_copy(
+                inc.at[:, plane, at], rows.at[k, pl.ds(HALF_ROWS * band + PREV, NEW)], l2.at[k, 1]
+            ),
+        )
+
+    barrier = pltpu.get_barrier_semaphore()
+    first, second = core == 0, core == 1
+
+    def greet(peer):
+        pl.semaphore_signal(barrier, inc=1, device_id=peer, device_id_type=MESH)
+
+    def tell(semaphore):
+        pl.semaphore_signal(semaphore, inc=1, device_id=twin, device_id_type=MESH)
+
+    @pl.when(second)
+    def _():
+        greet(twin)
+        greet((other, domain - 1))
+
+    @pl.when(first)
+    def _():
+        greet(partner)
+
+    for k in range(AHEAD):
+        for copy in stage(k):
+            copy.start()
+
+    @pl.when(first)
+    def _():
+        pl.semaphore_wait(barrier, 3)
+        tell(go)
+
+    @pl.when(second)
+    def _():
+        pl.semaphore_wait(go, 1)
+
+    def remote(src, dst, send, recv, peer):
+        return pltpu.make_async_remote_copy(
+            src_ref=src, dst_ref=dst, send_sem=send, recv_sem=recv,
+            device_id=peer, device_id_type=MESH,
+        )
+
+    def give(k):
+        return remote(
+            to_give.at[k], rows.at[k, pl.ds(HALF_ROWS * band, HALF_ROWS)],
+            s1.at[k], r1.at[k], partner,
+        )
+
+    for k in range(AHEAD):
+        for copy in stage(k):
+            copy.wait()
+        give(k).start()
+
+    def fetch(k, _):
+        for copy in own(k):
+            copy.start()
+
+        @pl.when(k + AHEAD < CHUNKS)
+        def _():
+            for copy in stage(k + AHEAD):
+                copy.start()
+
+        return 0
+
     x = ((domain // 2) % 2) * 2 + band
     y = (domain // 4) % 4
     z = domain // 16
-    other = 1 - band
 
     def device(xx, yy, zz, cc):
         return (xx % 2, ((zz * 4 + yy) * 2 + xx // 2) * 2 + cc)
 
     z_peers = [device(x, y, (z + d) % 4, core) for d in range(1, 4)]
     y_peers = [device(x, (y + d) % 4, z, core) for d in range(1, 4)]
-    partner = (other, domain)
-    twin = (band, domain + 1 - 2 * core)
     toward = 2 * core - 1
     early = (band + core + 1) % 2
     next_domain = (domain + toward + 64) % 64
@@ -122,88 +205,6 @@
     giver_domain = ((chip + ((x - way + 4) % 4) // 2) * 2 + band + way + 64) % 64
     chip_giver = (other, giver_domain - giver_domain % 2 + 1)
     early = early == 1
-
-    def piece(planes, k):
-        plane = planes + k // (CY // CHUNK_Y)
-        at = pl.multiple_of((k % (CY // CHUNK_Y)) * CHUNK_Y, CHUNK_Y)
-        return plane, pl.ds(at, CHUNK_Y)
-
-    def stage(k):
-        plane, at = piece(KEPT * other, k)
-        return (
-            pltpu.make_async_copy(earl.at[:, plane, at], to_give.at[k, 0:PREV], l1.at[k, 0]),
-            pltpu.make_async_copy(inc.at[:, plane, at], to_give.at[k, PREV:], l1.at[k, 1]),
-        )
-
-    def own(k):
-        plane, at = piece(KEPT * band, k)
-        return (
-            pltpu.make_async_copy(
-                earl.at[:, plane, at], rows.at[k, pl.ds(HALF_ROWS * band, PREV)], l2.at[k, 0]
-            ),
-            pltpu.make_async_copy(
-                inc.at[:, plane, at], rows.at[k, pl.ds(HALF_ROWS * band + PREV, NEW)], l2.at[k, 1]
-            ),
-        )
-
-    for k in range(AHEAD):
-        for copy in stage(k):
-            copy.start()
-
-    barrier = pltpu.get_barrier_semaphore()
-    first, second = core == 0, core == 1
-
-    def greet(peer):
-        pl.semaphore_signal(barrier, inc=1, device_id=peer, device_id_type=MESH)
-
-    def tell(semaphore):
-        pl.semaphore_signal(semaphore, inc=1, device_id=twin, device_id_type=MESH)
-
-    @pl.when(second)
-    def _():
-        greet(twin)
-        greet((other, domain - 1))
-
-    @pl.when(first)
-    def _():
-        greet(partner)
-
-    @pl.when(first)
-    def _():
-        pl.semaphore_wait(barrier, 3)
-        tell(go)
-
-    @pl.when(second)
-    def _():
-        pl.semaphore_wait(go, 1)
-
-    def remote(src, dst, send, recv, peer):
-        return pltpu.make_async_remote_copy(
-            src_ref=src, dst_ref=dst, send_sem=send, recv_sem=recv,
-            device_id=peer, device_id_type=MESH,
-        )
-
-    def give(k):
-        return remote(
-            to_give.at[k], rows.at[k, pl.ds(HALF_ROWS * band, HALF_ROWS)],
-            s1.at[k], r1.at[k], partner,
-        )
-
-    for k in range(AHEAD):
-        for copy in stage(k):
-            copy.wait()
-        give(k).start()
-
-    def fetch(k, _):
-        for copy in own(k):
-            copy.start()
-
-        @pl.when(k + AHEAD < CHUNKS)
-        def _():
-            for copy in stage(k + AHEAD):
-                copy.start()
-
-        return 0
 
     @pl.when(second)
     def _():

time: 223 us -> 223 us (level)
  no operation moved by 1% of the time
where the time goes in v9:
time: 223 us
  Pallas kernels  222 us (100%)
    pallas_call x1, Pallas kernels, on_device(): pl.pallas_call(kernel, out_shape=held, in_specs=[any_] * 4, out_specs=(in...  220 us

profile of v9, /device:TPU:1, one launch (start us, length us, event | category | flops | bytes accessed | tf_op | source)
XLA Modules:
  0.0 223.1 jit_solution(14744689837028299451)
XLA Ops:
  0.6 219.7 %shard_map.67 = (f32[16,8,32,128]{3,2,1,0:T(8,128)S(1)}, f32[64,64]{1,0:T(8,128)S(1)}, f32[32,8,32,128]{3,2,1,0:T(8,128)S(1)}) custom-call(f32[16,8,32,128]{3,2,1,0:T(8,128)} %orb.1, f32[8,32,128]{2,1,0:T(8,128)} %pot.1, f32[64,8,32,128]{3,2,1,0:T(8,128)} %earl.1, f32[32,8,32,128]{3,2,1,0:T(8,128)} %inc.1), custom_call_target="tpu_custom_call" | custom-call | flops 6000000000 | bytes 22000000 | tf_op jit(solution)/shard_map/pallas_call | solution.py:563
  220.3 2.7 %shard_map.68 = (f32[16,8,32,128]{3,2,1,0:T(8,128)}, f32[64,64]{1,0:T(8,128)}, f32[32,8,32,128]{3,2,1,0:T(8,128)}) custom-call(f32[16,8,32,128]{3,2,1,0:T(8,128)S(1)} %get-tuple-element.6.a, f32[64,64]{1,0:T(8,128)S(1)} %get-tuple-element.7.b, f32[32,8,32,128]{3,2,1,0:T(8,128)S(1)} %get-tuple-element.8.c), custom_call_target="tpu_custom_call" | custom-call | bytes 13000000 | tf_op jit(solution)/shard_map/pallas_call | solution.py:606

commit v10 on v5

--- a/solution.py
+++ b/solution.py
@@ -287,7 +287,7 @@
 
         @pl.when(jnp.logical_and(k == CHUNKS - 1, jnp.logical_not(early)))
         def _():
-            for copy in outer:
+            for copy in outer[1:]:
                 copy.start()
 
         @pl.when(jnp.logical_and(k == CHUNKS - 1, early))
@@ -308,6 +308,10 @@
         at = pl.ds(pl.multiple_of(base * CZ, CHUNK_Y * CZ), CHUNK_Y * CZ)
         hi, lo = high[:, at], low[:, at]
         grams[...] += nt(hi, hi) + nt(hi, lo) + nt(lo, hi)
+
+        @pl.when(jnp.logical_and(k == CHUNKS - 2, jnp.logical_not(early)))
+        def _():
+            outer[0].start()
 
         @pl.when(k < CHUNKS - 1)
         def _():

time: 226 us -> 223 us (0.987)
    pallas_call x1, Pallas kernels: 222 us -> 220 us  [on_device(): pl.pallas_call(kernel, out_shape=held, in_specs=[any_] * 4, out_specs=(in...]
where the time goes in v10:
time: 223 us
  Pallas kernels  223 us (100%)
    pallas_call x1, Pallas kernels, on_device(): pl.pallas_call(kernel, out_shape=held, in_specs=[any_] * 4, out_specs=(in...  220 us

profile of v10, /device:TPU:1, one launch (start us, length us, event | category | flops | bytes accessed | tf_op | source)
XLA Modules:
  0.0 223.2 jit_solution(4635168739446774616)
XLA Ops:
  0.6 219.8 %shard_map.67 = (f32[16,8,32,128]{3,2,1,0:T(8,128)S(1)}, f32[64,64]{1,0:T(8,128)S(1)}, f32[32,8,32,128]{3,2,1,0:T(8,128)S(1)}) custom-call(f32[16,8,32,128]{3,2,1,0:T(8,128)} %orb.1, f32[8,32,128]{2,1,0:T(8,128)} %pot.1, f32[64,8,32,128]{3,2,1,0:T(8,128)} %earl.1, f32[32,8,32,128]{3,2,1,0:T(8,128)} %inc.1), custom_call_target="tpu_custom_call" | custom-call | flops 6000000000 | bytes 22000000 | tf_op jit(solution)/shard_map/pallas_call | solution.py:566
  220.5 2.7 %shard_map.68 = (f32[16,8,32,128]{3,2,1,0:T(8,128)}, f32[64,64]{1,0:T(8,128)}, f32[32,8,32,128]{3,2,1,0:T(8,128)}) custom-call(f32[16,8,32,128]{3,2,1,0:T(8,128)S(1)} %get-tuple-element.6.a, f32[64,64]{1,0:T(8,128)S(1)} %get-tuple-element.7.b, f32[32,8,32,128]{3,2,1,0:T(8,128)S(1)} %get-tuple-element.8.c), custom_call_target="tpu_custom_call" | custom-call | bytes 13000000 | tf_op jit(solution)/shard_map/pallas_call | solution.py:609

commit v11 on v6

--- a/solution.py
+++ b/solution.py
@@ -41,7 +41,7 @@
 
 CHUNKS = 16
 CHUNK_Y = KEPT * CY // CHUNKS
-AHEAD = 2
+AHEAD = 3
 NEAR = -(-ORB // (CHUNKS - 1))
 PIECES = 4
 TILES = 16

time: 223 us -> 223 us (level)
  no operation moved by 1% of the time
where the time goes in v11:
time: 223 us
  Pallas kernels  223 us (100%)
    pallas_call x1, Pallas kernels, on_device(): pl.pallas_call(kernel, out_shape=held, in_specs=[any_] * 4, out_specs=(in...  220 us

profile of v11, /device:TPU:1, one launch (start us, length us, event | category | flops | bytes accessed | tf_op | source)
XLA Modules:
  0.0 223.2 jit_solution(1153212388593195139)
XLA Ops:
  0.6 219.8 %shard_map.67 = (f32[16,8,32,128]{3,2,1,0:T(8,128)S(1)}, f32[64,64]{1,0:T(8,128)S(1)}, f32[32,8,32,128]{3,2,1,0:T(8,128)S(1)}) custom-call(f32[16,8,32,128]{3,2,1,0:T(8,128)} %orb.1, f32[8,32,128]{2,1,0:T(8,128)} %pot.1, f32[64,8,32,128]{3,2,1,0:T(8,128)} %earl.1, f32[32,8,32,128]{3,2,1,0:T(8,128)} %inc.1), custom_call_target="tpu_custom_call" | custom-call | flops 6000000000 | bytes 22000000 | tf_op jit(solution)/shard_map/pallas_call | solution.py:562
  220.5 2.7 %shard_map.68 = (f32[16,8,32,128]{3,2,1,0:T(8,128)}, f32[64,64]{1,0:T(8,128)}, f32[32,8,32,128]{3,2,1,0:T(8,128)}) custom-call(f32[16,8,32,128]{3,2,1,0:T(8,128)S(1)} %get-tuple-element.6.a, f32[64,64]{1,0:T(8,128)S(1)} %get-tuple-element.7.b, f32[32,8,32,128]{3,2,1,0:T(8,128)S(1)} %get-tuple-element.8.c), custom_call_target="tpu_custom_call" | custom-call | bytes 13000000 | tf_op jit(solution)/shard_map/pallas_call | solution.py:605
